TPU v7x, 32 devices: a whole 2x2x4 slice. The times are simulated.
32 devices in a mesh: ta: 8 (over y, x, core), gx: 4 (over z).
Axes of the slice: x: 2, y: 2, z: 4, core: 2. Of those that a mesh axis runs over, the one named last changes fastest.
Arguments:
- eigenvectors: bfloat16 [16, 2, 32768, 3, 192], P('ta', None, 'gx'), may hold values from -6 to 6
- site_index: int32 [32768], P('gx'), may hold values from 0 to 32767, each once
- momenta: int32 [2, 3], replicated, may hold values from -3 to 3
- perambulators: bfloat16 [2, 16, 16, 768, 768], P(None, 'gx', 'ta'), may hold values from -6 to 6
- spin_perm: int32 [2, 4], replicated, may hold values from 0 to 3, each once within a row
- spin_sign: int32 [2, 4], replicated, may hold values from 0 to 1
Outputs:
- forward_box: bfloat16 [2, 16, 16, 768, 768], P(None, 'gx', 'ta')
- backward_box: bfloat16 [2, 16, 16, 768, 768], P(None, 'gx', 'ta')
Inputs may be any that keep to these rules, and one draw needn't show every extreme that they name: `site_index`: each lattice site appears exactly once. `spin_perm`: each row is a permutation of the spins.
All inputs are finite; a program needn't handle non-finite values.
Results may differ from a plain program's by a relative error of at most 0.008.
Values may be sent and summed in bfloat16 or wider, within the bound.
No kernel may reach another device: no remote copies, remote signals or barrier semaphores. Data moves between devices by JAX's collectives and lax.ppermute only.
A program may use at most 256 MiB of HBM per device.

v0:
```python
import math

import jax
import jax.numpy as jnp
from jax import lax
from jax.sharding import PartitionSpec as P

L = 32
NEV = 192
COLOR = 3
SITES = 32768


def from_root(value, axis, source):
    kept = jnp.where(lax.axis_index(axis) == source, value, 0).astype(value.dtype)
    return lax.psum(kept, axis)


def phases(site_index, momenta):
    first_coord = site_index // (L * L)
    second = site_index // L % L
    third_coord = site_index % L
    dotted = (
        momenta[:, 0:1] * first_coord[None, :]
        + momenta[:, 1:2] * second[None, :]
        + momenta[:, 2:3] * third_coord[None, :]
    )
    angles = jnp.mod(dotted, L).astype(jnp.float32) * (2.0 * math.pi / L)
    return (jnp.cos(angles), jnp.sin(angles))


def inner_rows(first_op, second_op):
    return lax.dot_general(
        first_op, second_op, (((0, 1), (0, 1)), ((), ())), preferred_element_type=jnp.float32
    )


def project(vectors, cosine, sine_value):
    real_part = vectors[0].astype(jnp.float32)
    imag_part = vectors[1].astype(jnp.float32)
    results = []
    for momentum in range(cosine.shape[0]):
        cosine_now = cosine[momentum][:, None, None]
        sine_now = sine_value[momentum][:, None, None]
        turned_real = (cosine_now * real_part - sine_now * imag_part).astype(jnp.bfloat16)
        turned_imag = (cosine_now * imag_part + sine_now * real_part).astype(jnp.bfloat16)
        real_out = inner_rows(vectors[0], turned_real) + inner_rows(vectors[1], turned_imag)
        imag_out = inner_rows(vectors[0], turned_imag) - inner_rows(vectors[1], turned_real)
        results.append(jnp.stack([real_out, imag_out]))
    return jnp.stack(results)


def spin_tables(spin_perm, spin_sign):
    spin_count = spin_perm.shape[1]
    matches = (
        spin_perm[:, :, None] == jnp.arange(spin_count, dtype=jnp.int32)[None, None, :]
    ).astype(jnp.float32)
    return matches * (2 * spin_sign - 1).astype(jnp.float32)[:, :, None]


def contract(form, first_op, second_op):
    return jnp.einsum(form, first_op, second_op, preferred_element_type=jnp.float32)


def complex_table(matrix):
    return jnp.stack([jnp.stack([matrix[0], -matrix[1]]), jnp.stack([matrix[1], matrix[0]])])


def pair_blocks(peram_block, sink_elems, source_elems, tables):
    spin_count = tables.shape[1]
    vector_count = sink_elems.shape[-1]
    dimension = spin_count * vector_count
    chiral = jnp.where(jnp.arange(spin_count) < spin_count // 2, 1.0, -1.0).astype(jnp.float32)
    blocks = peram_block.reshape(2, spin_count, vector_count, dimension)
    stacked = []
    for first_vertex, second_vertex in ((0, 1), (1, 0)):
        mixed_rows = contract(
            "rs,cslj->crlj", tables[first_vertex].astype(jnp.bfloat16), blocks
        ).astype(jnp.bfloat16)
        left_side = contract(
            "ockl,cslj->oskj", complex_table(sink_elems[first_vertex]), mixed_rows
        ).astype(jnp.bfloat16)
        left_side = left_side.reshape(2, dimension, spin_count, vector_count)
        signed = (tables[second_vertex] * chiral[None, :]).astype(jnp.bfloat16)
        turned = contract("cisk,sr->cirk", left_side, signed).astype(jnp.bfloat16)
        product = contract(
            "cisk,ockl->oisl", turned, complex_table(source_elems[second_vertex])
        ).astype(jnp.bfloat16)
        product = product.reshape(2, dimension, dimension)
        stacked.append(jnp.stack([product, jnp.stack([product[1], -product[0]])]))
    both_ways = jnp.stack(stacked)
    closed = contract("docim,cjm->doij", both_ways, peram_block)
    weights = jnp.repeat(chiral, vector_count) * (0.5 / math.sqrt(dimension))
    return (closed * weights).astype(jnp.bfloat16)


def on_device(eigenvectors, site_index, momenta, perambulators, spin_perm, spin_sign):
    cosine, sine_value = phases(site_index, momenta)
    local_times = eigenvectors.shape[0]
    partial_value = jnp.stack(
        [project(eigenvectors[position], cosine, sine_value) for position in range(local_times)]
    )
    summed = lax.psum(partial_value, "gx")
    elementals = (summed * (0.5 / math.sqrt(COLOR * SITES * NEV))).astype(jnp.bfloat16)
    sink_count = perambulators.shape[1]
    source_count = perambulators.shape[2]
    root_count = sink_count // local_times
    owned_parts = []
    for position in range(root_count):
        owned_parts.append(
            from_root(elementals, "ta", lax.axis_index("gx") * root_count + position)
        )
    sink_elems = jnp.concatenate(owned_parts, 0)
    tables = spin_tables(spin_perm, spin_sign)
    forward_rows = []
    backward_rows = []
    for sink_pos in range(sink_count):
        forward_cols = []
        backward_cols = []
        for source_pos in range(source_count):
            result = pair_blocks(
                perambulators[:, sink_pos, source_pos],
                sink_elems[sink_pos],
                elementals[source_pos],
                tables,
            )
            forward_cols.append(result[0])
            backward_cols.append(result[1])
        forward_rows.append(jnp.stack(forward_cols, 1))
        backward_rows.append(jnp.stack(backward_cols, 1))
    return (jnp.stack(forward_rows, 1), jnp.stack(backward_rows, 1))


def solution(mesh):
    return jax.shard_map(
        on_device,
        mesh=mesh,
        in_specs=(
            P("ta", None, "gx", None, None),
            P("gx"),
            P(),
            P(None, "gx", "ta", None, None),
            P(),
            P(),
        ),
        out_specs=(P(None, "gx", "ta", None, None), P(None, "gx", "ta", None, None)),
        check_vma=False,
    )
```

profile of v0, /device:TPU:0, one launch (start us, length us, event | category | flops | bytes accessed | tf_op | source)
XLA Modules:
  0.0 960.0 jit_solution(3743508751559863077)
XLA Ops:
  11.1 11.5 %fusion.452 = f32[192,192]{1,0:T(8,128)S(1)} fusion(bf16[2,2,8192,3,192]{2,4,3,1,0:T(8,128)(2,1)} %param.6, f32[8192]{0:T(1024)S(1)} %bitcast.1436, f32[8192]{0:T(1024)S(1)} %bitcast.1444), kind=kOutput, calls=%fused_computation.440 | convolution fusion | flops 1840250880 | bytes 28524544 | tf_op jit(solution)/shard_map/dot_general | solution.py:33
  22.5 11.2 %fusion.457 = f32[192,192]{1,0:T(8,128)S(1)} fusion(bf16[2,2,8192,3,192]{2,4,3,1,0:T(8,128)(2,1)} %param.6, f32[8192]{0:T(1024)S(1)} %bitcast.1437, f32[8192]{0:T(1024)S(1)} %bitcast.1445), kind=kOutput, calls=%fused_computation.441 | convolution fusion | flops 1840250880 | bytes 28524544 | tf_op jit(solution)/shard_map/dot_general | solution.py:33
  33.7 11.2 %fusion.462 = f32[192,192]{1,0:T(8,128)S(1)} fusion(bf16[2,2,8192,3,192]{2,4,3,1,0:T(8,128)(2,1)} %param.6, f32[8192]{0:T(1024)S(1)} %bitcast.1420, f32[8192]{0:T(1024)S(1)} %bitcast.1428), kind=kOutput, calls=%fused_computation.442 | convolution fusion | flops 1840250880 | bytes 28524544 | tf_op jit(solution)/shard_map/dot_general | solution.py:33
  44.9 11.2 %fusion.467 = f32[192,192]{1,0:T(8,128)S(1)} fusion(bf16[2,2,8192,3,192]{2,4,3,1,0:T(8,128)(2,1)} %param.6, f32[8192]{0:T(1024)S(1)} %bitcast.1421, f32[8192]{0:T(1024)S(1)} %bitcast.1429), kind=kOutput, calls=%fused_computation.443 | convolution fusion | flops 1840250880 | bytes 28524544 | tf_op jit(solution)/shard_map/dot_general | solution.py:33
  56.1 11.2 %fusion.532 = f32[192,192]{1,0:T(8,128)S(1)} fusion(bf16[2,2,8192,3,192]{2,4,3,1,0:T(8,128)(2,1)} %param.6, f32[8192]{0:T(1024)S(1)} %bitcast.1438, f32[8192]{0:T(1024)S(1)} %bitcast.1446), kind=kOutput, calls=%fused_computation.456 | convolution fusion | flops 1840250880 | bytes 28524544 | tf_op jit(solution)/shard_map/dot_general | solution.py:33
  67.2 11.7 %fusion.537 = f32[192,192]{1,0:T(8,128)S(1)} fusion(bf16[2,2,8192,3,192]{2,4,3,1,0:T(8,128)(2,1)} %param.6, f32[8192]{0:T(1024)S(1)} %bitcast.1439, f32[8192]{0:T(1024)S(1)} %bitcast.1447), kind=kOutput, calls=%fused_computation.457 | convolution fusion | flops 1840250880 | bytes 28524544 | tf_op jit(solution)/shard_map/dot_general | solution.py:33
  78.9 11.2 %fusion.542 = f32[192,192]{1,0:T(8,128)S(1)} fusion(bf16[2,2,8192,3,192]{2,4,3,1,0:T(8,128)(2,1)} %param.6, f32[8192]{0:T(1024)S(1)} %bitcast.1422, f32[8192]{0:T(1024)S(1)} %bitcast.1430), kind=kOutput, calls=%fused_computation.458 | convolution fusion | flops 1840250880 | bytes 28524544 | tf_op jit(solution)/shard_map/dot_general | solution.py:33
  90.1 11.2 %fusion.547 = f32[192,192]{1,0:T(8,128)S(1)} fusion(bf16[2,2,8192,3,192]{2,4,3,1,0:T(8,128)(2,1)} %param.6, f32[8192]{0:T(1024)S(1)} %bitcast.1423, f32[8192]{0:T(1024)S(1)} %bitcast.1431), kind=kOutput, calls=%fused_computation.459 | convolution fusion | flops 1840250880 | bytes 28524544 | tf_op jit(solution)/shard_map/dot_general | solution.py:33
  101.3 11.2 %fusion.402 = f32[1,192,192]{1,2,0:T(8,128)S(1)} fusion(f32[192,192]{1,0:T(8,128)S(1)} %fusion.452, bf16[2,2,8192,3,192]{2,4,3,1,0:T(8,128)(2,1)} %param.6, f32[8192]{0:T(1024)S(1)} %bitcast.1440, f32[8192]{0:T(1024)S(1)} %bitcast.1448), kind=kOutput, calls=%fused_computation.430 | convolution fusion | flops 1840287744 | bytes 28672000 | tf_op jit(solution)/shard_map/dot_general | solution.py:33
  112.5 11.2 %fusion.417 = f32[1,192,192]{1,2,0:T(8,128)S(1)} fusion(f32[192,192]{1,0:T(8,128)S(1)} %fusion.457, bf16[2,2,8192,3,192]{2,4,3,1,0:T(8,128)(2,1)} %param.6, f32[8192]{0:T(1024)S(1)} %bitcast.1441, f32[8192]{0:T(1024)S(1)} %bitcast.1449), kind=kOutput, calls=%fused_computation.433 | convolution fusion | flops 1840287744 | bytes 28672000 | tf_op jit(solution)/shard_map/dot_general | solution.py:33
  123.7 11.3 %fusion.432 = f32[1,192,192]{1,2,0:T(8,128)S(1)} fusion(f32[192,192]{1,0:T(8,128)S(1)} %fusion.462, bf16[2,2,8192,3,192]{2,4,3,1,0:T(8,128)(2,1)} %param.6, f32[8192]{0:T(1024)S(1)} %bitcast.1424, f32[8192]{0:T(1024)S(1)} %bitcast.1432), kind=kOutput, calls=%fused_computation.436 | convolution fusion | flops 1840287744 | bytes 28672000 | tf_op jit(solution)/shard_map/dot_general | solution.py:33
  135.0 11.2 %fusion.447 = f32[1,192,192]{1,2,0:T(8,128)S(1)} fusion(f32[192,192]{1,0:T(8,128)S(1)} %fusion.467, bf16[2,2,8192,3,192]{2,4,3,1,0:T(8,128)(2,1)} %param.6, f32[8192]{0:T(1024)S(1)} %bitcast.1425, f32[8192]{0:T(1024)S(1)} %bitcast.1433), kind=kOutput, calls=%fused_computation.439 | convolution fusion | flops 1840287744 | bytes 28672000 | tf_op jit(solution)/shard_map/dot_general | solution.py:33
  146.2 11.2 %fusion.482 = f32[1,192,192]{1,2,0:T(8,128)S(1)} fusion(f32[192,192]{1,0:T(8,128)S(1)} %fusion.532, bf16[2,2,8192,3,192]{2,4,3,1,0:T(8,128)(2,1)} %param.6, f32[8192]{0:T(1024)S(1)} %bitcast.1442, f32[8192]{0:T(1024)S(1)} %bitcast.1450), kind=kOutput, calls=%fused_computation.446 | convolution fusion | flops 1840287744 | bytes 28672000 | tf_op jit(solution)/shard_map/dot_general | solution.py:33
  157.4 11.2 %fusion.497 = f32[1,192,192]{1,2,0:T(8,128)S(1)} fusion(f32[192,192]{1,0:T(8,128)S(1)} %fusion.537, bf16[2,2,8192,3,192]{2,4,3,1,0:T(8,128)(2,1)} %param.6, f32[8192]{0:T(1024)S(1)} %bitcast.1443, f32[8192]{0:T(1024)S(1)} %bitcast.1451), kind=kOutput, calls=%fused_computation.449 | convolution fusion | flops 1840287744 | bytes 28672000 | tf_op jit(solution)/shard_map/dot_general | solution.py:33
  168.6 11.2 %fusion.512 = f32[1,192,192]{1,2,0:T(8,128)S(1)} fusion(f32[192,192]{1,0:T(8,128)S(1)} %fusion.542, bf16[2,2,8192,3,192]{2,4,3,1,0:T(8,128)(2,1)} %param.6, f32[8192]{0:T(1024)S(1)} %bitcast.1426, f32[8192]{0:T(1024)S(1)} %bitcast.1434), kind=kOutput, calls=%fused_computation.452 | convolution fusion | flops 1840287744 | bytes 28672000 | tf_op jit(solution)/shard_map/dot_general | solution.py:33
  179.7 11.2 %fusion.527 = f32[1,192,192]{1,2,0:T(8,128)S(1)} fusion(f32[192,192]{1,0:T(8,128)S(1)} %fusion.547, bf16[2,2,8192,3,192]{2,4,3,1,0:T(8,128)(2,1)} %param.6, f32[8192]{0:T(1024)S(1)} %bitcast.1427, f32[8192]{0:T(1024)S(1)} %bitcast.1435), kind=kOutput, calls=%fused_computation.455 | convolution fusion | flops 1840287744 | bytes 28672000 | tf_op jit(solution)/shard_map/dot_general | solution.py:33
  192.7 9.7 %fusion.610 = (bf16[2,1,1,768,768]{4,3,2,1,0:T(8,128)(2,1)}, bf16[2,1,1,768,768]{4,3,2,1,0:T(8,128)(2,1)}, bf16[2,1,1,768,768]{4,3,2,1,0:T(8,128)(2,1)S(1)}, bf1...) fusion(bf16[2,4,2,768,768]{4,3,2,1,0:T(8,128)(2,1)} %param.9), kind=kLoop, calls=%fused_computation.611 | loop fusion | bytes 37748736 | tf_op jit(solution)/shard_map/slice | solution.py:122
  270.8 55.6 %all-reduce.6.cloned.1.call-done = (bf16[2,2,2,192,192]{3,4,2,1,0:T(8,128)(2,1)}, bf16[2,2,2,192,192]{3,4,2,1,0:T(8,128)(2,1)}) async-done(((bf16[2,2,2,192,192]{3,4,2,1,0:T(8,128)(2,1)}, bf16[2,2,2,192,192]{3,4,2,1,0:T(8,128)(2,1)}), (bf16[2,2,2,192,192]{3,4,2,1,0:T(8,128)(2,1)}, bf16[2,2,2,192,192]{3,4,2,1,0:T(8,128)(2,1)})) %all-reduce.6.cloned.1.call-update) | async-done | bytes 1179664 | tf_op jit(solution)/shard_map/psum | solution.py:16
  392.9 9.8 %fusion.63 = bf16[2,2,768,768]{3,2,1,0:T(8,128)(2,1)S(1)} fusion(f32[768]{0:T(1024)S(1)} %mul.462, bf16[1,2,2,768,768]{4,3,2,1,0:T(8,128)(2,1)S(1)} %maximum_bitcast_fusion.1, bf16[1,2,2,768,768]{4,3,2,1,0:T(8,128)(2,1)S(1)} %maximum_bitcast_fusion, bf16[2,4,2,768,768]{4,3,2,1,0:T(8,128)(2,1)} %param.9), kind=kOutput, calls=%fused_computation.89 | convolution fusion | flops 7257194496 | bytes 16518144 | tf_op jit(solution)/shard_map/docim,cjm->doij/dot_general | solution.py:62
  437.0 6.3 reshape.656
  466.2 9.6 %fusion.62 = bf16[2,2,768,768]{3,2,1,0:T(8,128)(2,1)S(1)} fusion(f32[768]{0:T(1024)S(1)} %mul.462, bf16[1,2,2,768,768]{4,3,2,1,0:T(8,128)(2,1)S(1)} %maximum_bitcast_fusion.3, bf16[1,2,2,768,768]{4,3,2,1,0:T(8,128)(2,1)S(1)} %maximum_bitcast_fusion.2, bf16[2,4,2,768,768]{4,3,2,1,0:T(8,128)(2,1)} %param.9), kind=kOutput, calls=%fused_computation.87 | convolution fusion | flops 7257194496 | bytes 16518144 | tf_op jit(solution)/shard_map/docim,cjm->doij/dot_general | solution.py:62
  481.8 6.5 reshape.657
  539.5 9.6 %fusion.61 = bf16[2,2,768,768]{3,2,1,0:T(8,128)(2,1)S(1)} fusion(f32[768]{0:T(1024)S(1)} %mul.462, bf16[1,2,2,768,768]{4,3,2,1,0:T(8,128)(2,1)S(1)} %maximum_bitcast_fusion.6, bf16[1,2,2,768,768]{4,3,2,1,0:T(8,128)(2,1)S(1)} %maximum_bitcast_fusion.5, bf16[2,4,2,768,768]{4,3,2,1,0:T(8,128)(2,1)} %param.9), kind=kOutput, calls=%fused_computation.85 | convolution fusion | flops 7257194496 | bytes 16518144 | tf_op jit(solution)/shard_map/docim,cjm->doij/dot_general | solution.py:62
  612.5 10.0 %fusion.60 = bf16[2,2,768,768]{3,2,1,0:T(8,128)(2,1)S(1)} fusion(f32[768]{0:T(1024)S(1)} %mul.462, bf16[1,2,2,768,768]{4,3,2,1,0:T(8,128)(2,1)S(1)} %maximum_bitcast_fusion.8, bf16[1,2,2,768,768]{4,3,2,1,0:T(8,128)(2,1)S(1)} %maximum_bitcast_fusion.7, bf16[2,4,2,768,768]{4,3,2,1,0:T(8,128)(2,1)} %param.9), kind=kOutput, calls=%fused_computation.83 | convolution fusion | flops 7257194496 | bytes 16518144 | tf_op jit(solution)/shard_map/docim,cjm->doij/dot_general | solution.py:62
  686.2 9.6 %fusion.59 = bf16[2,2,768,768]{3,2,1,0:T(8,128)(2,1)S(1)} fusion(f32[768]{0:T(1024)S(1)} %mul.462, bf16[1,2,2,768,768]{4,3,2,1,0:T(8,128)(2,1)S(1)} %maximum_bitcast_fusion.11, bf16[1,2,2,768,768]{4,3,2,1,0:T(8,128)(2,1)S(1)} %maximum_bitcast_fusion.10, bf16[2,4,2,768,768]{4,3,2,1,0:T(8,128)(2,1)} %param.9), kind=kOutput, calls=%fused_computation.81 | convolution fusion | flops 7257194496 | bytes 16518144 | tf_op jit(solution)/shard_map/docim,cjm->doij/dot_general | solution.py:62
  759.2 10.0 %fusion.58 = bf16[2,2,768,768]{3,2,1,0:T(8,128)(2,1)S(1)} fusion(f32[768]{0:T(1024)S(1)} %mul.462, bf16[1,2,2,768,768]{4,3,2,1,0:T(8,128)(2,1)S(1)} %maximum_bitcast_fusion.13, bf16[1,2,2,768,768]{4,3,2,1,0:T(8,128)(2,1)S(1)} %maximum_bitcast_fusion.12, bf16[2,4,2,768,768]{4,3,2,1,0:T(8,128)(2,1)} %param.9), kind=kOutput, calls=%fused_computation.79 | convolution fusion | flops 7257194496 | bytes 16518144 | tf_op jit(solution)/shard_map/docim,cjm->doij/dot_general | solution.py:62
  803.6 6.2 reshape.666
  832.7 9.6 %fusion.57 = bf16[2,2,768,768]{3,2,1,0:T(8,128)(2,1)S(1)} fusion(f32[768]{0:T(1024)S(1)} %mul.462, bf16[1,2,2,768,768]{4,3,2,1,0:T(8,128)(2,1)S(1)} %maximum_bitcast_fusion.16, bf16[1,2,2,768,768]{4,3,2,1,0:T(8,128)(2,1)S(1)} %maximum_bitcast_fusion.15, bf16[2,4,2,768,768]{4,3,2,1,0:T(8,128)(2,1)} %param.9), kind=kOutput, calls=%fused_computation.77 | convolution fusion | flops 7257194496 | bytes 16518144 | tf_op jit(solution)/shard_map/docim,cjm->doij/dot_general | solution.py:62
  848.5 6.3 reshape.667
  905.5 9.6 fusion.56
  929.3 7.5 copy.171
  946.2 6.7 copy.170
  (570 shorter events, 581.4 us)
Async XLA Ops:
  7.2 257.3 %all-reduce.4.cloned.1.call-start = ((), (), s32[]{:S(2)}) async-start(), calls=%async_computation | async-start | bytes 3145728 | tf_op jit(solution)/shard_map/psum | solution.py:103
  192.5 133.9 %all-reduce.6.cloned.1.call-start = ((), (), s32[]{:S(2)}) async-start(), calls=%async_computation.1 | async-start | bytes 3145728 | tf_op jit(solution)/shard_map/psum | solution.py:16
  202.5 5.2 copy-start.55
  244.7 5.4 copy-start.54
  268.2 81.6 %copy-start.102 = (bf16[1,2,192,192]{2,3,1,0:T(8,128)(2,1)}, bf16[1,2,192,192]{2,3,1,0:T(8,128)(2,1)S(1)}, u32[]{:S(2)}) copy-start(bf16[1,2,192,192]{2,3,1,0:T(8,128)(2,1)S(1)} %get-tuple-element.119) | copy-start | bytes 442372
  268.2 81.6 %copy-start.106 = (bf16[1,2,192,192]{2,3,1,0:T(8,128)(2,1)}, bf16[1,2,192,192]{2,3,1,0:T(8,128)(2,1)S(1)}, u32[]{:S(2)}) copy-start(bf16[1,2,192,192]{2,3,1,0:T(8,128)(2,1)S(1)} %get-tuple-element.120) | copy-start | bytes 442372
  326.4 4.0 copy-start.56
  326.4 5.7 copy-start.151
  358.9 3.3 copy-start.130
  358.9 3.3 copy-start.132
  448.2 3.3 copy-start.82
  493.3 3.3 copy-start.107
  505.6 3.3 copy-start.134
  505.6 3.3 copy-start.136
  521.5 3.3 copy-start.99
  566.4 3.3 copy-start.91
  594.5 3.3 copy-start.83
  639.7 3.3 copy-start.108
  652.2 3.3 copy-start.138
  652.2 3.3 copy-start.140
  668.1 3.4 copy-start.96
  668.1 3.4 copy-start.100
  713.1 3.5 copy-start.88
  713.1 3.5 copy-start.92
  741.2 3.3 copy-start.84
  798.6 3.3 copy-start.126
  798.7 3.3 copy-start.128
  814.8 3.3 copy-start.101
  859.6 3.3 copy-start.93
  887.4 3.3 copy-start.85
  929.3 7.5 copy-start.16
  929.3 7.5 copy-start.18
  (122 other events, 282.6 us)
Sparse Core Ops, SparseCore 0:
  192.7 71.7 all-reduce.3
  268.2 58.1 all-reduce.5
where the time goes:
time: 966 us; the launch traced here: 960 us
  matrix products  427 us (44%)
  local copies, waits for them, and re-layouts  393 us (41%)
  other arithmetic  63.9 us (7%)
  waiting for transfers between devices  60.1 us (6%)
  between operations  16.4 us (2%)
    dot_general x72, matrix products, contract(): jnp.einsum(form, first_op, second_op, preferred_element_type=jnp.float32)  247 us
    dot_general x16, matrix products, inner_rows(): lax.dot_general(first_op, second_op, (((0, 1), (0, 1)), ((), ())), prefer...  180 us
    reshape x32, local copies, waits for them, and re-layouts, pair_blocks(): left_side = left_side.reshape(2, dimension, spin_count, vector_count)  177 us
    psum x1, waiting for transfers between devices, from_root(): return lax.psum(kept, axis)  55.6 us
    unnamed x306, local copies, waits for them, and re-layouts  54.3 us
    another operation x16, local copies, waits for them, and re-layouts, pair_blocks(): stacked.append(jnp.stack([product, jnp.stack([product[1], -product[0]])]))  39.9 us
    slice x16, local copies, waits for them, and re-layouts, pair_blocks(): stacked.append(jnp.stack([product, jnp.stack([product[1], -product[0]])]))  38.2 us
    convert_element_type x16, local copies, waits for them, and re-layouts, pair_blocks(): left_side = contract('ockl,cslj->oskj', complex_table(sink_elems[first_ve...  25.4 us
  transfers between devices with their start and end apart: 2, of which 2 were waited for; matrix products, arithmetic and copies ran while one was open for 7% of the time, Pallas kernels for 0%

commit v1 on v0

v1 whole, which is shorter than its diff:
```python
import functools
import math

import jax
import jax.numpy as jnp
import numpy as np
from jax import lax
from jax.experimental import pallas as pl
from jax.experimental.pallas import tpu as pltpu
from jax.sharding import PartitionSpec as P

F32, BF16 = jnp.float32, jnp.bfloat16
L = 32
VMEM_LIMIT = 58 * 2**20
BOTH_LAST = (((1,), (1,)), ((), ()))


def phases(site_index, momenta):
    first_coord = site_index // (L * L)
    second = site_index // L % L
    third_coord = site_index % L
    dotted = (
        momenta[:, 0:1] * first_coord[None, :]
        + momenta[:, 1:2] * second[None, :]
        + momenta[:, 2:3] * third_coord[None, :]
    )
    angles = jnp.mod(dotted, L).astype(F32) * (2.0 * math.pi / L)
    return (jnp.cos(angles), jnp.sin(angles))


def rows_dot(a, b):
    return jnp.dot(a, b, preferred_element_type=F32)


def cols_dot(a, b):
    return lax.dot_general(a, b, BOTH_LAST, preferred_element_type=F32)


def elemental_kernel(scale, sub, shares, here_ref, cos_ref, sin_ref, v_ref, *refs):
    outs, (acc, flat), turned = refs[:shares], refs[shares : shares + 2], refs[shares + 2 :]
    step = pl.program_id(0)
    nev, span = v_ref.shape[3], v_ref.shape[4]

    def turn(j, into):
        at = pl.ds(j * sub, sub)
        vr = v_ref[0, 0, 0, :, at].astype(F32)
        vi = v_ref[0, 1, 0, :, at].astype(F32)
        for p in range(2):
            c, s = cos_ref[p : p + 1, at], sin_ref[p : p + 1, at]
            into[pl.ds(2 * p * nev, nev), :] = (c * vr - s * vi).astype(BF16)
            into[pl.ds((2 * p + 1) * nev, nev), :] = (c * vi + s * vr).astype(BF16)

    @pl.when(step == 0)
    def _():
        acc[...] = jnp.zeros_like(acc)

    turn(0, turned[0])
    for j in range(span // sub):
        if (j + 1) * sub < span:
            turn(j + 1, turned[(j + 1) % 2])
        w = v_ref[0, :, 0, :, pl.ds(j * sub, sub)].reshape(2 * nev, sub)
        acc[...] += cols_dot(w, turned[j % 2][...])

    @pl.when(step == pl.num_programs(0) - 1)
    def _():
        for p in range(2):
            a, b, c = 2 * p * nev, (2 * p + 1) * nev, (2 * p + 2) * nev
            flat[pl.ds(a, nev), :] = (acc[:nev, a:b] + acc[nev:, b:c]) * scale
            flat[pl.ds(b, nev), :] = (acc[:nev, b:c] - acc[nev:, a:b]) * scale
        rows = 4 * nev // shares
        for k, out in enumerate(outs):
            share = lax.rem(here_ref[0] + k, shares)
            out[...] = flat[pl.ds(pl.multiple_of(share * rows, 16), rows), :].astype(out.dtype)


def elemental_shares(v, cosine, sine, here, shares, local, scale):
    _, _, colours, nev, sites = v.shape
    span = min(sites, 4096)
    sub = min(span, 1024)
    per = sites // span
    rows = 4 * nev // shares
    phase = pl.BlockSpec((2, span), lambda i: (0, i % per))
    whole = pl.BlockSpec((rows, nev), lambda i: (0, 0))
    return pl.pallas_call(
        functools.partial(elemental_kernel, scale, sub, shares),
        grid=(colours * per,),
        in_specs=[
            pl.BlockSpec(memory_space=pltpu.SMEM),
            phase,
            phase,
            pl.BlockSpec((1, 2, 1, nev, span), lambda i: (local, 0, i // per, 0, i % per)),
        ],
        out_specs=[whole] * shares,
        out_shape=[jax.ShapeDtypeStruct((rows, nev), F32 if k == 0 else BF16) for k in range(shares)],
        scratch_shapes=[pltpu.VMEM((2 * nev, 4 * nev), F32), pltpu.VMEM((4 * nev, nev), F32)]
        + [pltpu.VMEM((4 * nev, sub), BF16)] * 2,
        compiler_params=pltpu.CompilerParams(vmem_limit_bytes=VMEM_LIMIT),
        cost_estimate=pl.CostEstimate(
            flops=2 * 8 * nev * nev * colours * sites,
            bytes_accessed=4 * nev * colours * sites,
            transcendentals=0,
        ),
        name="elementals",
    )(here, cosine, sine, v)


def box_kernel(known, shares, locals_, has_base, pair_ref, here_ref, perm_ref, sign_ref, *refs):
    sinks = refs[:known]
    pieces = refs[known : known + known * shares]
    refs = refs[known + known * shares :]
    tau_ref = refs[0]
    refs = refs[3:] if has_base else refs[1:]
    fwd_ref, bwd_ref, ts, tab = refs[:4]
    lx = refs[4:]
    step = pl.program_id(0)
    nev = pieces[0].shape[-1]
    rows = pieces[0].shape[0]
    spins = perm_ref.shape[1]
    dim = spins * nev
    wide = tab.shape[-1]
    left, right = (lx[0:3], lx[3:6]), (lx[6:9], lx[9:12])
    tR, tI = tau_ref.at[0, 0, 0], tau_ref.at[1, 0, 0]
    sink, source = pair_ref[0, step], pair_ref[1, step]

    @pl.when(step == 0)
    def _():
        tab[...] = jnp.zeros_like(tab)

    def fill(side, p, er, ei):
        both = er.astype(F32) + (ei.astype(F32) if side == 0 else -ei.astype(F32))
        at = pl.ds(p * nev, nev)
        for k, e in enumerate((er, ei, both.astype(BF16))):
            tab[side, k, 0, at, 0:nev] = e
            tab[side, k, 1, at, wide - nev : wide] = e

    for t in range(known):

        @pl.when(lax.rem(sink, locals_) == t)
        def _():
            base = (sink // locals_) * (4 * nev)
            for p in range(2):
                er, ei = (
                    sinks[t][pl.ds(pl.multiple_of(base + (2 * p + c) * nev, 64), nev), :] for c in range(2)
                )
                fill(0, p, er, ei)

        @pl.when(source == t)
        def _():
            flat = left[0][0]
            for k in range(shares):
                share = lax.rem(here_ref[0] - k + shares, shares)
                flat[pl.ds(pl.multiple_of(share * rows, 16), rows), 0:nev] = pieces[t * shares + k][...]
            for p in range(2):
                er, ei = (flat[pl.ds((2 * p + c) * nev, nev), 0:nev] for c in range(2))
                fill(1, p, er, ei)

    ts[...] = (tR[...].astype(F32) + tI[...].astype(F32)).astype(BF16)
    taus = (tR, tI, ts)
    for s in range(spins):
        to, sign = [], []
        for p in range(2):
            at = jnp.int32(0)
            for r in range(1, spins):
                at = jnp.where(perm_ref[p, r] == s, r, at)
            to.append(pl.ds(pl.multiple_of(at * nev, 64), nev))
            sign.append((2 * sign_ref[p, at] - 1).astype(F32) * (1.0 if s < spins // 2 else -1.0))
        start = s * nev
        form, at = (0, start) if start + wide <= dim else (1, start + nev - wide)
        p1, p2, p3 = (rows_dot(tab[0, k, form], taus[k][pl.ds(at, wide), :]) for k in range(3))
        re = p1 - p2
        im = p3 - p1 - p2
        for k, x in enumerate((re, im, re + im)):
            for p in range(2):
                left[p][k][to[p], :] = x[p * nev : (p + 1) * nev].astype(BF16)
        form, at = (0, start) if start % 128 == 0 else (1, start + nev - wide)
        p1, p2, p3 = (cols_dot(tab[1, k, form], taus[k][:, pl.ds(at, wide)]) for k in range(3))
        re = p1 + p2
        im = p1 - p2 - p3
        for k, x in enumerate((re, im, re + im)):
            for p in range(2):
                right[1 - p][k][to[p], :] = (x[p * nev : (p + 1) * nev] * sign[p]).astype(BF16)

    tile = 256
    column = lax.broadcasted_iota(jnp.int32, (1, dim), 1)
    weight = jnp.where(column < dim // 2, 1.0, -1.0).astype(F32) * (0.5 / math.sqrt(dim))
    for d, out in ((0, fwd_ref), (1, bwd_ref)):
        for n in range(0, dim, tile):
            cols = pl.ds(n, tile)
            p1, p2, p3 = (rows_dot(left[d][k][...], right[d][k][:, cols]) for k in range(3))
            re = p1 - p2
            im = p3 - p1 - p2
            for r in range(spins):
                w = weight[:, n : n + tile] * (2 * sign_ref[d, r] - 1).astype(F32)
                block = slice(r * nev, (r + 1) * nev)
                out[0, 0, 0, block, cols] = (re[block] * w).astype(BF16)
                out[1, 0, 0, block, cols] = (im[block] * w).astype(BF16)


def boxes(pairs, here, perm, sign, sinks, pieces, tau, base, locals_):
    known, shares = len(sinks), len(pieces[0])
    _, _, _, dim, _ = tau.shape
    nev = pieces[0][0].shape[-1]
    smem = pl.BlockSpec(memory_space=pltpu.SMEM)
    big = pl.BlockSpec((2, 1, 1, dim, dim), lambda i, pair: (0, pair[0, i], pair[1, i], 0, 0))
    keep = pl.BlockSpec(memory_space=pl.ANY)
    small = lambda x: pl.BlockSpec(x.shape, lambda i, pair: (0, 0))
    flat = list(sinks) + [x for piece in pieces for x in piece]
    has_base = base is not None
    operands = [pairs, here, perm, sign] + flat + [tau] + (list(base) if has_base else [])
    count = pairs.shape[1]
    shape = jax.ShapeDtypeStruct(tau.shape, BF16)
    return pl.pallas_call(
        functools.partial(box_kernel, known, shares, locals_, has_base),
        grid_spec=pltpu.PrefetchScalarGridSpec(
            num_scalar_prefetch=1,
            grid=(count,),
            in_specs=[smem] * 3 + [small(x) for x in flat] + [big] + ([keep, keep] if has_base else []),
            out_specs=[big, big],
            scratch_shapes=[pltpu.VMEM((dim, dim), BF16), pltpu.VMEM((2, 3, 2, 2 * nev, 256), BF16)]
            + [pltpu.VMEM((dim, dim), BF16)] * 12,
        ),
        out_shape=[shape, shape],
        input_output_aliases={len(operands) - 2: 0, len(operands) - 1: 1} if has_base else {},
        compiler_params=pltpu.CompilerParams(vmem_limit_bytes=VMEM_LIMIT),
        cost_estimate=pl.CostEstimate(
            flops=count * 2 * 2 * (4 * dim**3 + 8 * dim * dim * nev),
            bytes_accessed=count * 12 * dim * dim,
            transcendentals=0,
        ),
        name="boxes",
    )(*operands)


def on_device(columns, rings, eigenvectors, site_index, momenta, perambulators, spin_perm, spin_sign):
    locals_, _, _, colours, nev = eigenvectors.shape
    roots = columns // rings
    cosine, sine = phases(site_index, momenta)
    v = jnp.transpose(eigenvectors, (0, 1, 3, 4, 2))
    here = lax.axis_index("gx").astype(jnp.int32).reshape(1)
    sites = eigenvectors.shape[2] * rings
    scale = 0.5 / math.sqrt(colours * sites * nev)
    sinks, pieces = [], []
    shift = lambda k: [(i, (i + k) % rings) for i in range(rings)]
    spread = [
        ((plane * roots + i) * rings + z, (i * rings + z) * rings + plane)
        for plane in range(rings)
        for i in range(roots)
        for z in range(rings)
    ]
    for local in range(locals_):
        parts = elemental_shares(v, cosine, sine, here, rings, local, scale)
        total = parts[0]
        for k in range(1, rings):
            total = total + lax.ppermute(parts[k], "gx", shift(k)).astype(F32)
        share = total.astype(BF16)
        pieces.append([share] + [lax.ppermute(share, "gx", shift(k)) for k in range(1, rings)])
        moved = lax.ppermute(share, ("ta", "gx"), spread)
        sinks.append(lax.all_gather(moved, "ta", tiled=True))
    base = None
    source_count = perambulators.shape[2]
    sink_count = perambulators.shape[1]
    for local in range(locals_):
        new = [
            (s, t)
            for t in range(source_count)
            for s in range(sink_count)
            if max(s % locals_, t) == local
        ]
        pairs = jnp.asarray(np.array(new, np.int32).T)
        base = boxes(
            pairs, here, spin_perm, spin_sign, sinks[: local + 1], pieces[: local + 1], perambulators, base, locals_
        )
    return tuple(base)


def solution(mesh):
    return jax.shard_map(
        functools.partial(on_device, mesh.shape["ta"], mesh.shape["gx"]),
        mesh=mesh,
        in_specs=(
            P("ta", None, "gx", None, None),
            P("gx"),
            P(),
            P(None, "gx", "ta", None, None),
            P(),
            P(),
        ),
        out_specs=(P(None, "gx", "ta", None, None), P(None, "gx", "ta", None, None)),
        check_vma=False,
    )
```

time: 966 us -> 200 us (0.21)
  matrix products: 427 us -> 0 us
  local copies, waits for them, and re-layouts: 393 us -> 3.81 us
  Pallas kernels: 0 us -> 135 us
  other arithmetic: 63.9 us -> 3.55 us
  waiting for transfers between devices: 60.1 us -> 7.92 us
  blocking collectives: 0 us -> 29.2 us
  starting transfers between devices: 0.08 us -> 18.8 us
  between operations: 16.4 us -> 0.77 us
    dot_general x88 -> x0, matrix products: 427 us -> none  [the longest x72 247 us: contract(): jnp.einsum(form, first_op, second_op, preferred_element_type=jnp.float32)]
    reshape x32 -> x0, local copies, waits for them, and re-layouts: 177 us -> none  [pair_blocks(): left_side = left_side.reshape(2, dimension, spin_count, vector_count)]
    pallas_call x0 -> x4, Pallas kernels: none -> 135 us  [the longest x2 95.7 us: boxes(): pl.pallas_call(functools.partial(box_kernel, known, shares, locals_, has_...]
    psum x2 -> x0, waiting for transfers between devices: 60 us -> none  [the longest x1 55.6 us: from_root(): return lax.psum(kept, axis)]
    another operation x24 -> x0, local copies, waits for them, and re-layouts: 59.4 us -> none  [the longest x16 39.9 us: pair_blocks(): stacked.append(jnp.stack([product, jnp.stack([product[1], -product[0]])]))]
    unnamed x306 -> x18, local copies, waits for them, and re-layouts: 54.3 us -> 1.33 us
    slice x19 -> x0, local copies, waits for them, and re-layouts: 48 us -> none  [the longest x16 38.2 us: pair_blocks(): stacked.append(jnp.stack([product, jnp.stack([product[1], -product[0]])]))]
    another operation x59 -> x0, other arithmetic: 36.6 us -> none  [the longest x16 14.8 us: pair_blocks(): stacked.append(jnp.stack([product, jnp.stack([product[1], -product[0]])]))]
  transfers between devices with their start and end apart: 2 -> 14, of which waited for: 2 -> 3; matrix products, arithmetic and copies ran while one was open for 7% -> 1% of each run, Pallas kernels for 0% -> 23%
where the time goes in v1:
time: 200 us; the launch traced here: 199 us
  Pallas kernels  135 us (68%)
  blocking collectives  29.2 us (15%)
  starting transfers between devices  18.8 us (9%)
  waiting for transfers between devices  7.92 us (4%)
  local copies, waits for them, and re-layouts  3.81 us (2%)
  other arithmetic  3.55 us (2%)
    pallas_call x2, Pallas kernels, boxes(): pl.pallas_call(functools.partial(box_kernel, known, shares, locals_, has_...  95.7 us
    pallas_call x2, Pallas kernels, elemental_shares(): pl.pallas_call(functools.partial(elemental_kernel, scale, sub, shares), g...  39.5 us
    all_gather x2, blocking collectives, on_device(): sinks.append(lax.all_gather(moved, 'ta', tiled=True))  29.2 us
    ppermute x6, starting transfers between devices, on_device(): total = total + lax.ppermute(parts[k], 'gx', shift(k)).astype(F32)  10.8 us
    ppermute x6, waiting for transfers between devices, on_device(): total = total + lax.ppermute(parts[k], 'gx', shift(k)).astype(F32)  7.9 us
    ppermute x6, starting transfers between devices, on_device(): lax.ppermute(share, 'gx', shift(k))  6.54 us
  transfers between devices with their start and end apart: 14, of which 3 were waited for; matrix products, arithmetic and copies ran while one was open for 1% of the time, Pallas kernels for 23%

profile of v1, /device:TPU:0, one launch (start us, length us, event | category | flops | bytes accessed | tf_op | source)
XLA Modules:
  0.0 199.3 jit_solution(15629529622330586844)
XLA Ops:
  0.6 1.0 slice_reduce_fusion.2
  1.6 0.8 add_select_fusion.3
  2.5 1.7 fusion.7
  4.2 1.5 cos.3.cos_ref
  5.6 19.7 %elementals.2 = (f32[192,192]{1,0:T(8,128)}, bf16[192,192]{1,0:T(8,128)(2,1)}, bf16[192,192]{1,0:T(8,128)(2,1)}, bf16[192,192]{1,0:T(8,128)(2,1)}) custom-call(s32[1]{0:T(128)} %bitcast.here_ref, f32[2,8192]{1,0:T(2,128)} %cos.3.cos_ref, f32[2,8192]{1,0:T(2,128)} %get-tuple-element.25.sin_ref, bf16[2,2,3,192,8192]{4,3,2,1,0:T(8,128)(2,1)} %bitcast.2), custom_call_target="tpu_custom_call" | custom-call | flops 14495514624 | bytes 18874368 | tf_op jit(solution)/shard_map/elementals/pallas_call | solution.py:84
  25.4 3.0 %collective-permute-start = (bf16[192,192]{1,0:T(8,128)(2,1)}, bf16[192,192]{1,0:T(8,128)(2,1)S(1)}, u32[]{:S(2)}, u32[]{:S(2)}) collective-permute-start(bf16[192,192]{1,0:T(8,128)(2,1)} %get-tuple-element.13), channel_id=1, source_target_pairs={{0,1},{1,2},{2,3},{3,0},{4,5},{5,6},{6,7},{7,4},{8,9},{9,10},{10,1... | collective-permute-start | bytes 221192 | tf_op jit(solution)/shard_map/ppermute | solution.py:254
  28.4 2.6 %collective-permute-start.1 = (bf16[192,192]{1,0:T(8,128)(2,1)}, bf16[192,192]{1,0:T(8,128)(2,1)S(1)}, u32[]{:S(2)}, u32[]{:S(2)}) collective-permute-start(bf16[192,192]{1,0:T(8,128)(2,1)} %get-tuple-element.14), channel_id=1, source_target_pairs={{0,2},{1,3},{2,0},{3,1},{4,6},{5,7},{6,4},{7,5},{8,10},{9,11},{10,... | collective-permute-start | bytes 221192 | tf_op jit(solution)/shard_map/ppermute | solution.py:254
  31.0 1.3 collective-permute-start.2
  32.3 19.7 %elementals.3 = (f32[192,192]{1,0:T(8,128)}, bf16[192,192]{1,0:T(8,128)(2,1)}, bf16[192,192]{1,0:T(8,128)(2,1)}, bf16[192,192]{1,0:T(8,128)(2,1)}) custom-call(s32[1]{0:T(128)} %bitcast.here_ref, f32[2,8192]{1,0:T(2,128)} %cos.3.cos_ref, f32[2,8192]{1,0:T(2,128)} %get-tuple-element.25.sin_ref, bf16[2,2,3,192,8192]{4,3,2,1,0:T(8,128)(2,1)} %bitcast.3), custom_call_target="tpu_custom_call" | custom-call | flops 14495514624 | bytes 18874368 | tf_op jit(solution)/shard_map/elementals/pallas_call | solution.py:84
  52.1 0.7 collective-permute-start.4
  52.7 0.3 collective-permute-start.5
  53.1 2.8 %collective-permute-start.6 = (bf16[192,192]{1,0:T(8,128)(2,1)}, bf16[192,192]{1,0:T(8,128)(2,1)S(1)}, u32[]{:S(2)}, u32[]{:S(2)}) collective-permute-start(bf16[192,192]{1,0:T(8,128)(2,1)} %get-tuple-element.19), channel_id=1, source_target_pairs={{0,3},{1,0},{2,1},{3,2},{4,7},{5,4},{6,5},{7,6},{8,11},{9,8},{10,9... | collective-permute-start | bytes 221192 | tf_op jit(solution)/shard_map/ppermute | solution.py:254
  56.0 0.7 collective-permute-start.3
  56.6 3.2 %collective-permute-done.4 = bf16[192,192]{1,0:T(8,128)(2,1)S(1)} collective-permute-done((bf16[192,192]{1,0:T(8,128)(2,1)}, bf16[192,192]{1,0:T(8,128)(2,1)S(1)}, u32[]{:S(2)}, u32[]{:S(2)}) %collective-permute-start.4) | collective-permute-done | bytes 73760 | tf_op jit(solution)/shard_map/ppermute | solution.py:254
  59.9 2.3 %collective-permute-done.5 = bf16[192,192]{1,0:T(8,128)(2,1)S(1)} collective-permute-done((bf16[192,192]{1,0:T(8,128)(2,1)}, bf16[192,192]{1,0:T(8,128)(2,1)S(1)}, u32[]{:S(2)}, u32[]{:S(2)}) %collective-permute-start.5) | collective-permute-done | bytes 73760 | tf_op jit(solution)/shard_map/ppermute | solution.py:254
  62.1 2.4 %collective-permute-done.6 = bf16[192,192]{1,0:T(8,128)(2,1)S(1)} collective-permute-done((bf16[192,192]{1,0:T(8,128)(2,1)}, bf16[192,192]{1,0:T(8,128)(2,1)S(1)}, u32[]{:S(2)}, u32[]{:S(2)}) %collective-permute-start.6) | collective-permute-done | bytes 73760 | tf_op jit(solution)/shard_map/ppermute | solution.py:254
  64.5 1.0 add_convert_fusion.refs_6_
  65.5 0.1 collective-permute-start.13
  65.6 3.8 %collective-permute-start.12 = (bf16[192,192]{1,0:T(8,128)(2,1)S(1)}, bf16[192,192]{1,0:T(8,128)(2,1)S(1)}, u32[]{:S(2)}, u32[]{:S(2)}) collective-permute-start(bf16[192,192]{1,0:T(8,128)(2,1)S(1)} %add_convert_fusion.refs_6_), channel_id=1, source_target_pairs={{0,2},{1,3},{2,0},{3,1},{4,6},{5,7},{6,4},{7,5},{8,10},{9,11},{10,... | collective-permute-start | bytes 221192 | tf_op jit(solution)/shard_map/ppermute | solution.py:256
  69.4 1.0 collective-permute-start.10
  70.4 0.1 collective-permute-start.9
  70.5 0.9 collective-permute-start.8
  71.5 13.2 %all_gather.6.refs_0_ = bf16[1536,192]{1,0:T(8,128)(2,1)} all-gather(bf16[192,192]{1,0:T(8,128)(2,1)S(1)} %collective-permute-done.3), channel_id=1, replica_groups=mesh['ta'=8,'gx'=4] {'ta'}, dimensions={0}, use_global_device_ids=true | all-gather | bytes 663552 | tf_op jit(solution)/shard_map/all_gather | solution.py:258
  84.6 0.6 collective-permute-start.11
  85.3 0.8 collective-permute-start.7
  86.1 0.6 copy-done.7
  86.8 26.3 %boxes.2 = (bf16[2,4,2,768,768]{4,3,2,1,0:T(8,128)(2,1)}, bf16[2,4,2,768,768]{4,3,2,1,0:T(8,128)(2,1)}) custom-call(s32[2,2]{1,0:T(2,128)} %constant.62.clone.pair_ref, s32[1]{0:T(128)} %bitcast.here_ref, s32[2,4]{1,0:T(2,128)} %perm_ref.3, s32[2,4]{1,0:T(2,128)} %sign_ref.3, bf16[1536,192]{1,0:T(8,128)(2,1)} %all_gather.6.refs_0_, ...), custom_call_target="tpu_custom_call" | custom-call | flops 21743271936 | bytes 14155776 | tf_op jit(solution)/shard_map/boxes/pallas_call | solution.py:212
  113.0 16.1 %all_gather.7.refs_1_ = bf16[1536,192]{1,0:T(8,128)(2,1)} all-gather(bf16[192,192]{1,0:T(8,128)(2,1)S(1)} %collective-permute-done.7), channel_id=1, replica_groups=mesh['ta'=8,'gx'=4] {'ta'}, dimensions={0}, use_global_device_ids=true | all-gather | bytes 663552 | tf_op jit(solution)/shard_map/all_gather | solution.py:258
  129.1 0.6 copy-done.3
  129.7 0.0 copy-done.4
  129.8 0.0 copy-done.8
  129.8 69.5 %boxes.3 = (bf16[2,4,2,768,768]{4,3,2,1,0:T(8,128)(2,1)}, bf16[2,4,2,768,768]{4,3,2,1,0:T(8,128)(2,1)}) custom-call(s32[2,6]{1,0:T(2,128)} %constant.63.clone.pair_ref, s32[1]{0:T(128)} %bitcast.here_ref, s32[2,4]{1,0:T(2,128)} %perm_ref.3, s32[2,4]{1,0:T(2,128)} %sign_ref.3, ...), custom_call_target="tpu_custom_call", output_to_operand_aliasing={{0}: (15, {}), {1}: (16, {})} | custom-call | flops 65229815808 | bytes 42467328 | tf_op jit(solution)/shard_map/boxes/pallas_call | solution.py:212
  (26 shorter events, 0.1 us)
Async XLA Ops:
  25.4 27.7 %collective-permute-start = (bf16[192,192]{1,0:T(8,128)(2,1)}, bf16[192,192]{1,0:T(8,128)(2,1)S(1)}, u32[]{:S(2)}, u32[]{:S(2)}) collective-permute-start(bf16[192,192]{1,0:T(8,128)(2,1)} %get-tuple-element.13), channel_id=1, source_target_pairs={{0,1},{1,2},{2,3},{3,0},{4,5},{5,6},{6,7},{7,4},{8,9},{9,10},{10,1... | collective-permute-start | bytes 221192 | tf_op jit(solution)/shard_map/ppermute | solution.py:254
  28.4 27.5 %collective-permute-start.1 = (bf16[192,192]{1,0:T(8,128)(2,1)}, bf16[192,192]{1,0:T(8,128)(2,1)S(1)}, u32[]{:S(2)}, u32[]{:S(2)}) collective-permute-start(bf16[192,192]{1,0:T(8,128)(2,1)} %get-tuple-element.14), channel_id=1, source_target_pairs={{0,2},{1,3},{2,0},{3,1},{4,6},{5,7},{6,4},{7,5},{8,10},{9,11},{10,... | collective-permute-start | bytes 221192 | tf_op jit(solution)/shard_map/ppermute | solution.py:254
  31.0 24.9 %copy-start = (f32[192,192]{1,0:T(8,128)S(1)}, f32[192,192]{1,0:T(8,128)}, u32[]{:S(2)}) copy-start(f32[192,192]{1,0:T(8,128)} %get-tuple-element.12) | copy-start | bytes 442372
  31.0 24.9 %collective-permute-start.2 = (bf16[192,192]{1,0:T(8,128)(2,1)}, bf16[192,192]{1,0:T(8,128)(2,1)S(1)}, u32[]{:S(2)}, u32[]{:S(2)}) collective-permute-start(bf16[192,192]{1,0:T(8,128)(2,1)} %get-tuple-element.15), channel_id=1, source_target_pairs={{0,3},{1,0},{2,1},{3,2},{4,7},{5,4},{6,5},{7,6},{8,11},{9,8},{10,9... | collective-permute-start | bytes 221192 | tf_op jit(solution)/shard_map/ppermute | solution.py:254
  52.1 7.8 %collective-permute-start.4 = (bf16[192,192]{1,0:T(8,128)(2,1)}, bf16[192,192]{1,0:T(8,128)(2,1)S(1)}, u32[]{:S(2)}, u32[]{:S(2)}) collective-permute-start(bf16[192,192]{1,0:T(8,128)(2,1)} %get-tuple-element.17), channel_id=1, source_target_pairs={{0,1},{1,2},{2,3},{3,0},{4,5},{5,6},{6,7},{7,4},{8,9},{9,10},{10,1... | collective-permute-start | bytes 221192 | tf_op jit(solution)/shard_map/ppermute | solution.py:254
  52.7 9.4 %collective-permute-start.5 = (bf16[192,192]{1,0:T(8,128)(2,1)}, bf16[192,192]{1,0:T(8,128)(2,1)S(1)}, u32[]{:S(2)}, u32[]{:S(2)}) collective-permute-start(bf16[192,192]{1,0:T(8,128)(2,1)} %get-tuple-element.18), channel_id=1, source_target_pairs={{0,2},{1,3},{2,0},{3,1},{4,6},{5,7},{6,4},{7,5},{8,10},{9,11},{10,... | collective-permute-start | bytes 221192 | tf_op jit(solution)/shard_map/ppermute | solution.py:254
  53.1 11.5 %collective-permute-start.6 = (bf16[192,192]{1,0:T(8,128)(2,1)}, bf16[192,192]{1,0:T(8,128)(2,1)S(1)}, u32[]{:S(2)}, u32[]{:S(2)}) collective-permute-start(bf16[192,192]{1,0:T(8,128)(2,1)} %get-tuple-element.19), channel_id=1, source_target_pairs={{0,3},{1,0},{2,1},{3,2},{4,7},{5,4},{6,5},{7,6},{8,11},{9,8},{10,9... | collective-permute-start | bytes 221192 | tf_op jit(solution)/shard_map/ppermute | solution.py:254
  56.0 30.1 %copy-start.1 = (bf16[192,192]{1,0:T(8,128)(2,1)}, bf16[192,192]{1,0:T(8,128)(2,1)S(1)}, u32[]{:S(2)}) copy-start(bf16[192,192]{1,0:T(8,128)(2,1)S(1)} %add_convert_fusion.1.refs_1_.refs_2_) | copy-start | bytes 221188
  56.0 14.6 %collective-permute-start.3 = (bf16[192,192]{1,0:T(8,128)(2,1)S(1)}, bf16[192,192]{1,0:T(8,128)(2,1)S(1)}, u32[]{:S(2)}, u32[]{:S(2)}) collective-permute-start(bf16[192,192]{1,0:T(8,128)(2,1)S(1)} %add_convert_fusion.1.refs_1_.refs_2_), channel_id=1, source_target_pairs={{0,0},{1,4},{2,8},{3,12},{4,16},{5,20},{6,24},{7,28},{8,1},{9,5},{... | collective-permute-start | bytes 221192 | tf_op jit(solution)/shard_map/ppermute | solution.py:257
  65.5 47.5 %copy-start.2 = (bf16[192,192]{1,0:T(8,128)(2,1)}, bf16[192,192]{1,0:T(8,128)(2,1)S(1)}, u32[]{:S(2)}) copy-start(bf16[192,192]{1,0:T(8,128)(2,1)S(1)} %add_convert_fusion.refs_6_) | copy-start | bytes 221188
  65.5 63.6 %collective-permute-start.13 = (bf16[192,192]{1,0:T(8,128)(2,1)S(1)}, bf16[192,192]{1,0:T(8,128)(2,1)S(1)}, u32[]{:S(2)}, u32[]{:S(2)}) collective-permute-start(bf16[192,192]{1,0:T(8,128)(2,1)S(1)} %add_convert_fusion.refs_6_), channel_id=1, source_target_pairs={{0,3},{1,0},{2,1},{3,2},{4,7},{5,4},{6,5},{7,6},{8,11},{9,8},{10,9... | collective-permute-start | bytes 221192 | tf_op jit(solution)/shard_map/ppermute | solution.py:256
  65.6 63.5 %collective-permute-start.12 = (bf16[192,192]{1,0:T(8,128)(2,1)S(1)}, bf16[192,192]{1,0:T(8,128)(2,1)S(1)}, u32[]{:S(2)}, u32[]{:S(2)}) collective-permute-start(bf16[192,192]{1,0:T(8,128)(2,1)S(1)} %add_convert_fusion.refs_6_), channel_id=1, source_target_pairs={{0,2},{1,3},{2,0},{3,1},{4,6},{5,7},{6,4},{7,5},{8,10},{9,11},{10,... | collective-permute-start | bytes 221192 | tf_op jit(solution)/shard_map/ppermute | solution.py:256
  69.4 15.2 %collective-permute-start.10 = (bf16[192,192]{1,0:T(8,128)(2,1)S(1)}, bf16[192,192]{1,0:T(8,128)(2,1)S(1)}, u32[]{:S(2)}, u32[]{:S(2)}) collective-permute-start(bf16[192,192]{1,0:T(8,128)(2,1)S(1)} %add_convert_fusion.1.refs_1_.refs_2_), channel_id=1, source_target_pairs={{0,3},{1,0},{2,1},{3,2},{4,7},{5,4},{6,5},{7,6},{8,11},{9,8},{10,9... | collective-permute-start | bytes 221192 | tf_op jit(solution)/shard_map/ppermute | solution.py:256
  70.4 14.8 %collective-permute-start.9 = (bf16[192,192]{1,0:T(8,128)(2,1)S(1)}, bf16[192,192]{1,0:T(8,128)(2,1)S(1)}, u32[]{:S(2)}, u32[]{:S(2)}) collective-permute-start(bf16[192,192]{1,0:T(8,128)(2,1)S(1)} %add_convert_fusion.1.refs_1_.refs_2_), channel_id=1, source_target_pairs={{0,2},{1,3},{2,0},{3,1},{4,6},{5,7},{6,4},{7,5},{8,10},{9,11},{10,... | collective-permute-start | bytes 221192 | tf_op jit(solution)/shard_map/ppermute | solution.py:256
  70.5 15.6 %collective-permute-start.8 = (bf16[192,192]{1,0:T(8,128)(2,1)S(1)}, bf16[192,192]{1,0:T(8,128)(2,1)S(1)}, u32[]{:S(2)}, u32[]{:S(2)}) collective-permute-start(bf16[192,192]{1,0:T(8,128)(2,1)S(1)} %add_convert_fusion.1.refs_1_.refs_2_), channel_id=1, source_target_pairs={{0,1},{1,2},{2,3},{3,0},{4,5},{5,6},{6,7},{7,4},{8,9},{9,10},{10,1... | collective-permute-start | bytes 221192 | tf_op jit(solution)/shard_map/ppermute | solution.py:256
  84.6 1.5 copy-start.5
  84.6 44.5 %collective-permute-start.11 = (bf16[192,192]{1,0:T(8,128)(2,1)S(1)}, bf16[192,192]{1,0:T(8,128)(2,1)S(1)}, u32[]{:S(2)}, u32[]{:S(2)}) collective-permute-start(bf16[192,192]{1,0:T(8,128)(2,1)S(1)} %add_convert_fusion.refs_6_), channel_id=1, source_target_pairs={{0,1},{1,2},{2,3},{3,0},{4,5},{5,6},{6,7},{7,4},{8,9},{9,10},{10,1... | collective-permute-start | bytes 221192 | tf_op jit(solution)/shard_map/ppermute | solution.py:256
  85.2 0.9 copy-start.6
  85.3 27.8 %collective-permute-start.7 = (bf16[192,192]{1,0:T(8,128)(2,1)S(1)}, bf16[192,192]{1,0:T(8,128)(2,1)S(1)}, u32[]{:S(2)}, u32[]{:S(2)}) collective-permute-start(bf16[192,192]{1,0:T(8,128)(2,1)S(1)} %add_convert_fusion.refs_6_), channel_id=1, source_target_pairs={{0,0},{1,4},{2,8},{3,12},{4,16},{5,20},{6,24},{7,28},{8,1},{9,5},{... | collective-permute-start | bytes 221192 | tf_op jit(solution)/shard_map/ppermute | solution.py:257
  86.1 0.6 copy-start.7
  129.1 0.6 copy-start.3
  129.1 0.7 copy-start.4
  129.1 0.7 copy-start.8
